TPU v7x, 256 devices: a whole 4x4x8 slice. The times are simulated.
256 devices in a mesh: slab: 32 (over z, y_lo, core), harm: 8 (over x, y_hi).
Axes of the slice: x: 4, y: 4 (y_hi: 2, y_lo: 2; y = y_hi * 2 + y_lo), z: 8, core: 2. Of those that a mesh axis runs over, the one named last changes fastest.
Arguments:
- adjoint: float32 [64, 3, 32, 128, 128], P('harm', None, 'slab'), may hold values from -6 to 6
- jacobian: bfloat16 [3, 3, 128, 32, 128, 128], P(None, None, None, 'slab', 'harm'), may hold values from -0.9 to 6, as said below
- conductivity: float32 [32, 128, 128], P('slab'), may hold values from 0.2 to 2
- harm_order: int32 [32], replicated, may hold values from 1 to 63, as said below
Outputs:
- first_image: float32 [64, 3, 32, 128, 128], P('harm', None, 'slab')
- second_image: float32 [64, 3, 32, 128, 128], P('harm', None, 'slab')
Inputs may be any that keep to these rules, and one draw needn't show every extreme that they name: `jacobian`: saved reluctivity Jacobians, three by three for each time sample and cell. `harm_order`: each of the first 32 odd numbers once.
All inputs are finite; a program needn't handle non-finite values.
Results may differ from a plain program's by a relative error of at most 0.0086.
Values may be sent and summed in bfloat16 or wider, within the bound.
A program may use at most 64 MiB of HBM per device.

v0:
```python
import math

import jax
import jax.numpy as jnp
from jax import lax
from jax.sharding import PartitionSpec as P

H = 32
NT = 128


def padded_2(cells, sides, width):
    for axis, dim in sides:
        count = lax.axis_size(axis)
        ends = count - 1
        head = lax.slice_in_dim(cells, 0, width, axis=dim)
        tail = lax.slice_in_dim(cells, cells.shape[dim] - width, cells.shape[dim], axis=dim)
        cells = jnp.concatenate(
            [
                lax.ppermute(tail, axis, [(i, (i + 1) % count) for i in range(ends)]),
                cells,
                lax.ppermute(head, axis, [((i + 1) % count, i) for i in range(ends)]),
            ],
            axis=dim,
        )
    return cells


def build_table(harm_order, steps):
    sample_ids = jnp.arange(steps, dtype=jnp.int32)
    phases = harm_order[:, None] * sample_ids[None, :] % steps
    angles = phases.astype(jnp.float32) * (2.0 * math.pi / steps)
    paired = jnp.stack([jnp.cos(angles), jnp.sin(angles)], axis=1)
    return paired.reshape(-1, steps).astype(jnp.bfloat16)


def inplane_sum(values):
    padded = jnp.pad(values, ((0, 0), (0, 0), (0, 0), (1, 1), (1, 1)))
    beside = padded[:, :, :, 2:, 1:-1] + padded[:, :, :, :-2, 1:-1]
    return beside + padded[:, :, :, 1:-1, 2:] + padded[:, :, :, 1:-1, :-2]


def axial_planes(returned):
    extended = padded_2(returned, (("slab", 2),), 1)
    upper = extended[:, :, 2:].astype(jnp.float32)
    lower = extended[:, :, :-2].astype(jnp.float32)
    return upper + lower


def weigh_samples(jacobian, samples):
    weighted = []
    for comp_out in range(3):
        total = jnp.zeros(samples[:, 0].shape, jnp.float32)
        for comp_in in range(3):
            total = total + jacobian[comp_in, comp_out].astype(jnp.float32) * samples[
                :, comp_in
            ].astype(jnp.float32)
        weighted.append(total)
    return jnp.stack(weighted, axis=1).astype(jnp.bfloat16)


def reluct_cells(packed, jacobian, table):
    samples = jnp.dot(
        table.T, packed.reshape(packed.shape[0], -1), preferred_element_type=jnp.float32
    )
    samples = samples.astype(jnp.bfloat16).reshape((NT, 3) + packed.shape[2:])
    weighted = weigh_samples(jacobian, samples)
    coeffs = jnp.dot(table, weighted.reshape(NT, -1), preferred_element_type=jnp.float32) * (
        2.0 / NT
    )
    return coeffs.astype(jnp.bfloat16).reshape((table.shape[0], 3) + weighted.shape[2:])


def shards(adjoint, jacobian, conductivity, harm_order):
    table = build_table(harm_order, NT)
    local_coeffs = adjoint.shape[0]
    offset = lax.axis_index("harm") * local_coeffs
    orders = lax.dynamic_slice_in_dim(harm_order, offset // 2, local_coeffs // 2, 0).astype(
        jnp.float32
    ) / (2.0 * H)
    factor = orders.reshape(-1, 1, 1, 1, 1) * conductivity[None, None]

    def transposed_apply(adjoint_in):
        packed = adjoint_in.astype(jnp.bfloat16)
        moved = lax.all_to_all(packed, "harm", split_axis=3, concat_axis=0, tiled=True)
        coeffs = reluct_cells(moved, jacobian, table)
        returned = lax.all_to_all(coeffs, "harm", split_axis=0, concat_axis=3, tiled=True)
        paired = adjoint_in.reshape((local_coeffs // 2, 2) + adjoint_in.shape[1:])
        eddy_term = jnp.stack([factor * paired[:, 1], -factor * paired[:, 0]], axis=1).reshape(
            adjoint_in.shape
        )
        axial_sum = axial_planes(returned)
        center = returned.astype(jnp.float32)
        return 0.25 * (6.0 * center - inplane_sum(center) - axial_sum) + eddy_term

    first_image = transposed_apply(adjoint)
    second_image = transposed_apply(first_image)
    return (first_image, second_image)


def solution(mesh):
    return jax.shard_map(
        shards,
        mesh=mesh,
        in_specs=(
            P("harm", None, "slab", None, None),
            P(None, None, None, "slab", "harm", None),
            P("slab", None, None),
            P(),
        ),
        out_specs=(P("harm", None, "slab", None, None), P("harm", None, "slab", None, None)),
        check_vma=False,
    )
```

profile of v0, /device:TPU:225, one launch (start us, length us, event | category | flops | bytes accessed | tf_op | source)
XLA Modules:
  0.0 146.6 jit_solution(16174963664761380797)
XLA Ops:
  0.6 3.2 %copy.215 = bf16[8,3,1,128,128]{4,0,2,1,3:T(8,128)(2,1)} copy(f32[8,3,1,128,128]{4,3,2,1,0:T(8,128)} %param.4) | data formatting | bytes 2359296 | tf_op args[0]
  3.8 6.7 %all-to-all-start = ((bf16[8,3,1,128,128]{4,0,2,1,3:T(8,128)(2,1)}), bf16[8,3,1,128,128]{4,0,2,1,3:T(8,128)(2,1)S(1)}, u32[]{:S(2)}, u32[]{:S(2)}) async-start(bf16[8,3,1,128,128]{4,0,2,1,3:T(8,128)(2,1)} %copy.215), calls=%async_computation | async-start | bytes 1572864 | tf_op jit(solution)/shard_map/all_to_all | solution.py:85
  10.7 4.2 %fusion.46 = (bf16[1,1,128,1,16,128]{5,4,3,2,1,0:T(8,128)(2,1)}, bf16[1,1,128,1,16,128]{5,4,3,2,1,0:T(8,128)(2,1)}, bf16[1,1,128,1,16,128]{5,4,3,2,1,0:T(8,128)(...) fusion(bf16[3,3,128,1,16,128]{5,4,3,2,1,0:T(8,128)(2,1)} %param.5), kind=kLoop, calls=%fused_computation.94 | loop fusion | bytes 9437184 | tf_op jit(solution)/shard_map/slice | solution.py:55
  14.9 2.2 %copy.203 = bf16[1,1,128,1,16,128]{2,5,4,3,1,0:T(8,128)(2,1)} copy(bf16[1,1,128,1,16,128]{5,4,3,2,1,0:T(8,128)(2,1)} %get-tuple-element.16) | data formatting | bytes 1048576
  17.2 2.2 %copy.210 = bf16[1,1,128,1,16,128]{2,5,4,3,1,0:T(8,128)(2,1)} copy(bf16[1,1,128,1,16,128]{5,4,3,2,1,0:T(8,128)(2,1)} %get-tuple-element.17) | data formatting | bytes 1048576
  19.4 2.2 %copy.209 = bf16[1,1,128,1,16,128]{2,5,4,3,1,0:T(8,128)(2,1)} copy(bf16[1,1,128,1,16,128]{5,4,3,2,1,0:T(8,128)(2,1)} %get-tuple-element.18) | data formatting | bytes 1048576
  21.6 2.2 %copy.208 = bf16[1,1,128,1,16,128]{2,5,4,3,1,0:T(8,128)(2,1)} copy(bf16[1,1,128,1,16,128]{5,4,3,2,1,0:T(8,128)(2,1)} %get-tuple-element.19) | data formatting | bytes 1048576
  23.9 1.2 copy.207
  25.1 1.2 copy.206
  26.3 1.2 copy.205
  27.5 1.2 copy.204
  28.8 1.2 copy.211
  31.3 0.9 copy.201
  32.2 3.6 %fusion.21 = (bf16[128,1,1,16,128]{0,4,3,1,2:T(8,128)(2,1)S(1)}, bf16[128,1,1,16,128]{0,4,3,1,2:T(8,128)(2,1)S(1)}, bf16[128,1,1,16,128]{0,4,3,1,2:T(8,128)(2,1)S(1)}) fusion(bf16[1,1,128,1,16,128]{2,5,4,3,1,0:T(8,128)(2,1)} %copy.205, bf16[1,1,128,1,16,128]{2,5,4,3,1,0:T(8,128)(2,1)} %copy.204, bf16[1,1,128,1,16,128]{2,5,4,3,1,0:T(8,128)(2,1)} %copy.203, ...), kind=kLoop, calls=%fused_computation.56 | loop fusion | flops 7864320 | bytes 7864320 | tf_op jit(solution)/shard_map/convert.12
  36.6 1.0 copy.212
  37.6 6.8 %all-to-all-start.1 = ((bf16[64,3,1,16,128]{4,3,1,2,0:T(8,128)(2,1)}), bf16[64,3,1,16,128]{4,3,1,2,0:T(8,128)(2,1)S(1)}, u32[]{:S(2)}, u32[]{:S(2)}) async-start(bf16[64,3,1,16,128]{4,3,1,2,0:T(8,128)(2,1)} %bitcast.13), calls=%async_computation.1 | async-start | bytes 1572864 | tf_op jit(solution)/shard_map/all_to_all | solution.py:87
  44.5 12.4 %all-to-all-done.1 = bf16[64,3,1,16,128]{4,3,1,2,0:T(8,128)(2,1)S(1)} async-done(((bf16[64,3,1,16,128]{4,3,1,2,0:T(8,128)(2,1)}), bf16[64,3,1,16,128]{4,3,1,2,0:T(8,128)(2,1)S(1)}, u32[]{:S(2)}, u32[]{:S(2)}) %all-to-all-start.1) | async-done | bytes 786464 | tf_op jit(solution)/shard_map/all_to_all | solution.py:87
  57.1 3.8 %collective-permute-start = (bf16[8,3,1,128,128]{4,3,1,0,2:T(8,128)(2,1)S(1)}, bf16[8,3,1,128,128]{4,3,1,0,2:T(8,128)(2,1)S(1)}, u32[]{:S(2)}, u32[]{:S(2)}) collective-permute-start(bf16[8,3,1,128,128]{4,3,1,0,2:T(8,128)(2,1)S(1)} %bitcast.109), channel_id=1, source_target_pairs={{8,0},{16,8},{24,16},{32,24},{40,32},{48,40},{56,48},{64,56},{72,6... | collective-permute-start | bytes 2359304 | tf_op jit(solution)/shard_map/ppermute | solution.py:22
  60.9 2.4 %collective-permute-start.1 = (bf16[8,3,1,128,128]{4,3,1,0,2:T(8,128)(2,1)S(1)}, bf16[8,3,1,128,128]{4,3,1,0,2:T(8,128)(2,1)S(1)}, u32[]{:S(2)}, u32[]{:S(2)}) collective-permute-start(bf16[8,3,1,128,128]{4,3,1,0,2:T(8,128)(2,1)S(1)} %bitcast.110), channel_id=1, source_target_pairs={{0,8},{8,16},{16,24},{24,32},{32,40},{40,48},{48,56},{56,64},{64,7... | collective-permute-start | bytes 2359304 | tf_op jit(solution)/shard_map/ppermute | solution.py:20
  64.4 19.0 %collective-permute-done = bf16[8,3,1,128,128]{4,3,1,0,2:T(8,128)(2,1)S(1)} collective-permute-done((bf16[8,3,1,128,128]{4,3,1,0,2:T(8,128)(2,1)S(1)}, bf16[8,3,1,128,128]{4,3,1,0,2:T(8,128)(2,1)S(1)}, u32[]{:S(2)}, u32[]{:S(2)}) %collective-permute-start) | collective-permute-done | bytes 786464 | tf_op jit(solution)/shard_map/ppermute | solution.py:22
  83.5 1.1 fusion.44
  85.1 14.0 %all_to_all.66 = bf16[8,3,1,128,128]{4,0,2,1,3:T(8,128)(2,1)S(1)} all-to-all(bf16[8,3,1,128,128]{4,0,2,1,3:T(8,128)(2,1)S(1)} %copy.191), channel_id=1, replica_groups=mesh['slab'=32,'harm'=8] {'harm'}, dimensions={3} | all-to-all | bytes 1572864 | tf_op jit(solution)/shard_map/all_to_all | solution.py:85
  99.5 1.2 reshape.530
  100.7 1.7 %convolution_convert_fusion = bf16[128,6144]{1,0:T(8,128)(2,1)S(1)} fusion(bf16[64,128]{1,0:T(8,128)(2,1)S(1)} %bitcast.115, bf16[64,6144]{1,0:T(8,128)(2,1)} %reshape.530), kind=kOutput, calls=%fused_computation | convolution fusion | flops 101449728 | bytes 2375680 | tf_op jit(solution)/shard_map/dot_general | solution.py:63
  102.4 1.6 %copy.202 = bf16[128,6144]{0,1:T(8,128)(2,1)} copy(bf16[128,6144]{1,0:T(8,128)(2,1)S(1)} %convolution_convert_fusion) | data formatting | bytes 3145728 | tf_op jit(solution)/shard_map/reshape | solution.py:66
  104.0 4.0 %fusion.30 = (bf16[128,1,1,16,128]{0,4,3,1,2:T(8,128)(2,1)S(1)}, bf16[128,1,1,16,128]{0,4,3,1,2:T(8,128)(2,1)S(1)}, bf16[128,1,1,16,128]{0,4,3,1,2:T(8,128)(2,1)S(1)}) fusion(bf16[1,1,128,1,16,128]{2,5,4,3,1,0:T(8,128)(2,1)} %copy.205, bf16[1,1,128,1,16,128]{2,5,4,3,1,0:T(8,128)(2,1)} %copy.204, bf16[1,1,128,1,16,128]{2,5,4,3,1,0:T(8,128)(2,1)} %copy.203, ...), kind=kLoop, calls=%fused_computation.65 | loop fusion | flops 7864320 | bytes 7864320 | tf_op jit(solution)/shard_map/convert.9
  108.2 0.7 fusion.17
  109.0 12.8 %all_to_all.67 = bf16[64,3,1,16,128]{4,3,1,2,0:T(8,128)(2,1)S(1)} all-to-all(bf16[64,3,1,16,128]{4,3,1,2,0:T(8,128)(2,1)S(1)} %bitcast.107), channel_id=1, replica_groups=mesh['slab'=32,'harm'=8] {'harm'}, dimensions={0} | all-to-all | bytes 1572864 | tf_op jit(solution)/shard_map/all_to_all | solution.py:87
  122.0 1.9 %collective-permute-start.2 = (bf16[8,3,1,128,128]{4,3,1,0,2:T(8,128)(2,1)S(1)}, bf16[8,3,1,128,128]{4,3,1,0,2:T(8,128)(2,1)S(1)}, u32[]{:S(2)}, u32[]{:S(2)}) collective-permute-start(bf16[8,3,1,128,128]{4,3,1,0,2:T(8,128)(2,1)S(1)} %bitcast.111), channel_id=1, source_target_pairs={{8,0},{16,8},{24,16},{32,24},{40,32},{48,40},{56,48},{64,56},{72,6... | collective-permute-start | bytes 2359304 | tf_op jit(solution)/shard_map/ppermute | solution.py:22
  124.0 4.0 %collective-permute-start.3 = (bf16[8,3,1,128,128]{4,3,1,0,2:T(8,128)(2,1)S(1)}, bf16[8,3,1,128,128]{4,3,1,0,2:T(8,128)(2,1)S(1)}, u32[]{:S(2)}, u32[]{:S(2)}) collective-permute-start(bf16[8,3,1,128,128]{4,3,1,0,2:T(8,128)(2,1)S(1)} %bitcast.112), channel_id=1, source_target_pairs={{0,8},{8,16},{16,24},{24,32},{32,40},{40,48},{48,56},{56,64},{64,7... | collective-permute-start | bytes 2359304 | tf_op jit(solution)/shard_map/ppermute | solution.py:20
  128.5 15.7 %collective-permute-done.2 = bf16[8,3,1,128,128]{4,3,1,0,2:T(8,128)(2,1)S(1)} collective-permute-done((bf16[8,3,1,128,128]{4,3,1,0,2:T(8,128)(2,1)S(1)}, bf16[8,3,1,128,128]{4,3,1,0,2:T(8,128)(2,1)S(1)}, u32[]{:S(2)}, u32[]{:S(2)}) %collective-permute-start.2) | collective-permute-done | bytes 786464 | tf_op jit(solution)/shard_map/ppermute | solution.py:22
  144.1 2.4 %fusion.16 = f32[8,3,1,128,128]{4,3,2,1,0:T(8,128)} fusion(f32[8,3,1,128,128]{4,3,1,0,2:T(8,128)S(1)} %bitcast.101, f32[8,3,1,128,128]{4,3,1,0,2:T(8,128)S(1)} %bitcast_convert_fusion, bf16[8,3,1,128,128]{4,3,1,0,2:T(8,128)(2,1)S(1)} %collective-permute-done.3, bf16[8,3,1,128,128]{4,3,1,0,2:T(8,128)(2,1)S(1)} %collective-permute-done.2), kind=kLoop, calls=%fused_computation.28 | loop fusion | flops 4325376 | bytes 6291456
  (39 shorter events, 5.5 us)
Async XLA Ops:
  0.6 9.9 %copy-start.5 = (s32[32]{0:T(128)S(1)}, s32[32]{0:T(128)}, u32[]{:S(2)}) copy-start(s32[32]{0:T(128)} %param.7) | copy-start | bytes 388
  3.8 26.1 %all-to-all-start = ((bf16[8,3,1,128,128]{4,0,2,1,3:T(8,128)(2,1)}), bf16[8,3,1,128,128]{4,0,2,1,3:T(8,128)(2,1)S(1)}, u32[]{:S(2)}, u32[]{:S(2)}) async-start(bf16[8,3,1,128,128]{4,0,2,1,3:T(8,128)(2,1)} %copy.215), calls=%async_computation | async-start | bytes 1572864 | tf_op jit(solution)/shard_map/all_to_all | solution.py:85
  37.6 25.7 %copy-start.4 = (f32[1,128,128]{2,1,0:T(8,128)S(1)}, f32[1,128,128]{2,1,0:T(8,128)}, u32[]{:S(2)}) copy-start(f32[1,128,128]{2,1,0:T(8,128)} %param.6) | copy-start | bytes 196612
  37.6 25.8 %copy-start.1 = (f32[8,3,1,128,128]{4,3,2,1,0:T(8,128)S(1)}, f32[8,3,1,128,128]{4,3,2,1,0:T(8,128)}, u32[]{:S(2)}) copy-start(f32[8,3,1,128,128]{4,3,2,1,0:T(8,128)} %param.4) | copy-start | bytes 4718596
  37.6 19.3 %all-to-all-start.1 = ((bf16[64,3,1,16,128]{4,3,1,2,0:T(8,128)(2,1)}), bf16[64,3,1,16,128]{4,3,1,2,0:T(8,128)(2,1)S(1)}, u32[]{:S(2)}, u32[]{:S(2)}) async-start(bf16[64,3,1,16,128]{4,3,1,2,0:T(8,128)(2,1)} %bitcast.13), calls=%async_computation.1 | async-start | bytes 1572864 | tf_op jit(solution)/shard_map/all_to_all | solution.py:87
  57.1 26.4 %collective-permute-start = (bf16[8,3,1,128,128]{4,3,1,0,2:T(8,128)(2,1)S(1)}, bf16[8,3,1,128,128]{4,3,1,0,2:T(8,128)(2,1)S(1)}, u32[]{:S(2)}, u32[]{:S(2)}) collective-permute-start(bf16[8,3,1,128,128]{4,3,1,0,2:T(8,128)(2,1)S(1)} %bitcast.109), channel_id=1, source_target_pairs={{8,0},{16,8},{24,16},{32,24},{40,32},{48,40},{56,48},{64,56},{72,6... | collective-permute-start | bytes 2359304 | tf_op jit(solution)/shard_map/ppermute | solution.py:22
  60.9 22.6 %collective-permute-start.1 = (bf16[8,3,1,128,128]{4,3,1,0,2:T(8,128)(2,1)S(1)}, bf16[8,3,1,128,128]{4,3,1,0,2:T(8,128)(2,1)S(1)}, u32[]{:S(2)}, u32[]{:S(2)}) collective-permute-start(bf16[8,3,1,128,128]{4,3,1,0,2:T(8,128)(2,1)S(1)} %bitcast.110), channel_id=1, source_target_pairs={{0,8},{8,16},{16,24},{24,32},{32,40},{40,48},{48,56},{56,64},{64,7... | collective-permute-start | bytes 2359304 | tf_op jit(solution)/shard_map/ppermute | solution.py:20
  63.4 0.7 copy-start.2
  84.6 43.4 %copy-start = (f32[8,3,1,128,128]{4,3,1,0,2:T(8,128)}, f32[8,3,1,128,128]{4,3,1,0,2:T(8,128)S(1)}, u32[]{:S(2)}) copy-start(f32[8,3,1,128,128]{4,3,1,0,2:T(8,128)S(1)} %get-tuple-element.15) | copy-start | bytes 4718596
  109.0 19.0 %copy-start.3 = (f32[4,128,128]{2,1,0:T(8,128)S(1)}, f32[4,128,128]{2,1,0:T(8,128)}, u32[]{:S(2)}) copy-start(f32[4,128,128]{2,1,0:T(8,128)} %copy-done.2) | copy-start | bytes 786436
  122.0 22.1 %collective-permute-start.2 = (bf16[8,3,1,128,128]{4,3,1,0,2:T(8,128)(2,1)S(1)}, bf16[8,3,1,128,128]{4,3,1,0,2:T(8,128)(2,1)S(1)}, u32[]{:S(2)}, u32[]{:S(2)}) collective-permute-start(bf16[8,3,1,128,128]{4,3,1,0,2:T(8,128)(2,1)S(1)} %bitcast.111), channel_id=1, source_target_pairs={{8,0},{16,8},{24,16},{32,24},{40,32},{48,40},{56,48},{64,56},{72,6... | collective-permute-start | bytes 2359304 | tf_op jit(solution)/shard_map/ppermute | solution.py:22
  124.0 20.2 %collective-permute-start.3 = (bf16[8,3,1,128,128]{4,3,1,0,2:T(8,128)(2,1)S(1)}, bf16[8,3,1,128,128]{4,3,1,0,2:T(8,128)(2,1)S(1)}, u32[]{:S(2)}, u32[]{:S(2)}) collective-permute-start(bf16[8,3,1,128,128]{4,3,1,0,2:T(8,128)(2,1)S(1)} %bitcast.112), channel_id=1, source_target_pairs={{0,8},{8,16},{16,24},{24,32},{32,40},{40,48},{48,56},{56,64},{64,7... | collective-permute-start | bytes 2359304 | tf_op jit(solution)/shard_map/ppermute | solution.py:20
where the time goes:
time: 147 us
  waiting for transfers between devices  47.1 us (32%)
  local copies, waits for them, and re-layouts  29.8 us (20%)
  blocking collectives  26.8 us (18%)
  starting transfers between devices  25.5 us (17%)
  other arithmetic  12.8 us (9%)
  matrix products  3.64 us (2%)
    ppermute x2, waiting for transfers between devices, padded_2(): lax.ppermute(head, axis, [((i + 1) % count, i) for i in range(ends)])  34.7 us
    unnamed x24, local copies, waits for them, and re-layouts  20 us
    all_to_all x1, blocking collectives, transposed_apply(): lax.all_to_all(packed, 'harm', split_axis=3, concat_axis=0, tiled=True)  14 us
    all_to_all x1, blocking collectives, transposed_apply(): lax.all_to_all(coeffs, 'harm', split_axis=0, concat_axis=3, tiled=True)  12.8 us
    all_to_all x1, waiting for transfers between devices, transposed_apply(): lax.all_to_all(coeffs, 'harm', split_axis=0, concat_axis=3, tiled=True)  12.4 us
    another operation x3, other arithmetic  7.78 us
    all_to_all x1, starting transfers between devices, transposed_apply(): lax.all_to_all(coeffs, 'harm', split_axis=0, concat_axis=3, tiled=True)  6.77 us
    all_to_all x1, starting transfers between devices, transposed_apply(): lax.all_to_all(packed, 'harm', split_axis=3, concat_axis=0, tiled=True)  6.65 us
  transfers between devices with their start and end apart: 6, of which 3 were waited for; matrix products, arithmetic and copies ran while one was open for 14% of the time, Pallas kernels for 0%

commit v1 on v0

v1 whole, which is shorter than its diff:
```python
import math

import jax
import jax.numpy as jnp
from jax import lax
from jax.experimental import pallas as pl
from jax.experimental.pallas import tpu as pltpu
from jax.sharding import PartitionSpec as P

H = 32
NT = 128
HALF = NT // 2
C = 2 * H
R = 8
K = C * R
MESH = pl.DeviceIdType.MESH
F32 = jnp.float32
BF16 = jnp.bfloat16


def kernel(
    adj_hbm, jac_hbm, cond_hbm, orders_hbm,
    out1, out2,
    adj, cond, orders, mat, pk, x1, jac, jeff, tf, tb, wgt, cf, c1, zm, zo, xs, xr, x2, r1, e1, m1, c2, r2, e2, m2,
    fac1, fac2, my, ms, mc, mh, mf,
    jsem, adj_sem, cond_sem, ord_sem, a_s, a_r, z_s, z_r, x_s, x_r, f_s, f_r, o_s, o_r, e_s, e_r, m_s, m_r,
    fa_s, fa_r, fc_s, fc_r, n_s, n_r,
):
    p = lax.axis_index("slab")
    h = lax.axis_index("harm")
    planes = lax.axis_size("slab")
    n = lax.axis_size("harm")
    odd = lax.rem(p, 2)
    mate = p + 1 - 2 * odd
    outer = p - 1 + 2 * odd
    has_outer = jnp.logical_and(outer >= 0, outer < planes)

    def peer(k):
        return lax.rem(h + k, n)

    def rdma(src, dst, ss, rs, dev):
        return pltpu.make_async_remote_copy(
            src_ref=src, dst_ref=dst, send_sem=ss, recv_sem=rs, device_id=dev, device_id_type=MESH
        )

    def adj_copy(q):
        part = pl.ds(2 * q, 2)
        return pltpu.make_async_copy(adj_hbm.at[part], adj.at[part], adj_sem.at[q])

    for q in range(4):
        adj_copy(q).start()
    ord_copy = pltpu.make_async_copy(orders_hbm, orders, ord_sem)
    ord_copy.start()
    cond_copy = pltpu.make_async_copy(cond_hbm, cond, cond_sem)
    cond_copy.start()
    jcopy = pltpu.make_async_copy(jac_hbm, jac, jsem)
    jcopy.start()

    hx, hy = h // 2, lax.rem(h, 2)

    def at(dx, y):
        return 2 * lax.rem(hx + dx + 4, 4) + y

    def flip_dst(dx):
        return at(dx, 1 - hy)

    DIRECT = (2, 1, 3)
    FLIPS = (2, 1, 3, 0)

    barrier = pltpu.get_barrier_semaphore()
    for k in range(1, n):
        pl.semaphore_signal(barrier, inc=1, device_id=(p, peer(k)), device_id_type=MESH)
    pl.semaphore_signal(barrier, inc=1, device_id=(mate, h), device_id_type=MESH)

    @pl.when(has_outer)
    def _():
        for k in range(n):
            pl.semaphore_signal(barrier, inc=1, device_id=(outer, peer(k)), device_id_type=MESH)

    for q in range(4):
        adj_copy(q).wait()

        def pack(g, _, q=q):
            rows = pl.ds(pl.multiple_of(g * R, R), R)
            for i in range(3):
                both = jnp.concatenate([adj[2 * q, i, 0, rows, :], adj[2 * q + 1, i, 0, rows, :]], axis=0)
                pk[g, i, q] = both.astype(BF16)
            return 0

        lax.fori_loop(0, 2 * n, pack, 0, unroll=4)

    pl.semaphore_wait(barrier, n + n * has_outer.astype(jnp.int32))

    def a2a(g, dx):
        dst = at(dx, hy)
        return rdma(pk.at[2 * dst + g], x1.at[g, :, pl.ds(4 * h, 4)], a_s.at[g, dx], a_r.at[g, dx], (p, dst))

    def a2a_flip(g, dx):
        dst = flip_dst(dx)
        return rdma(pk.at[2 * dst + g], x1.at[g, :, pl.ds(4 * h, 4)], fa_s.at[g, dx], fa_r.at[g, dx], (p, dst))

    for g in range(2):
        for dx in FLIPS:
            a2a_flip(g, dx).start()
        for dx in DIRECT:
            a2a(g, dx).start()

    for g in range(2):
        x1[g, :, pl.ds(4 * h, 4)] = pk[2 * h + g]

    ord_copy.wait()
    for k in range(H):
        mat[2 * k:2 * k + 2, :] = jnp.full((2, 128), orders[k], jnp.int32)
    steps = lax.broadcasted_iota(jnp.int32, (C, 128), 1)
    quarter = (lax.broadcasted_iota(jnp.int32, (C, 128), 0) & 1) * (NT // 4)
    phases = (mat[...] * steps + (NT - quarter)) & (NT - 1)
    tab = jnp.cos(phases.astype(F32) * (2.0 * math.pi / NT))[:, :HALF].astype(BF16)

    def iota(shape, dim):
        return lax.broadcasted_iota(jnp.int32, shape, dim)

    def spread(dims, dst):
        cols = ((iota((C, K), 1) >> 3) == iota((C, K), 0)).astype(F32).astype(BF16)
        rows = ((iota((K, C), 0) >> 3) == iota((K, C), 1)).astype(F32).astype(BF16)
        mid = lax.dot_general(rows, tab, dims, preferred_element_type=F32).astype(BF16)
        full = jnp.dot(mid, cols, preferred_element_type=F32)
        same = ((iota((K, K), 0) ^ iota((K, K), 1)) & (R - 1)) == 0
        dst[...] = jnp.where(same, full, 0.0).astype(BF16)

    spread((((1,), (1,)), ((), ())), tf)
    spread((((1,), (0,)), ((), ())), tb)


    QUARTER = 0.25

    def fill(dst, *terms):
        total = jnp.zeros(dst.shape, F32)
        for where, value in terms:
            total = jnp.where(where, value, total)
        dst[...] = total.astype(BF16)

    ya, yb = iota((128, 128), 0), iota((128, 128), 1)
    fill(my, (ya == yb, 6.0 * QUARTER), (jnp.abs(ya - yb) == 1, -QUARTER))
    sa, sb = iota((256, 256), 0), iota((256, 256), 1)
    alike = (sa >> 3) == (sb >> 3)
    fill(ms, (jnp.logical_and(alike, jnp.abs(sa - sb) == 1), -QUARTER))
    fill(mc.at[0], (jnp.logical_and(alike, sa - sb == R - 1), -QUARTER))
    fill(mc.at[1], (jnp.logical_and(alike, sb - sa == R - 1), -QUARTER))
    ha, hb = iota((256, 32), 0), iota((256, 32), 1)
    fill(mh.at[0], (ha == hb * R, -QUARTER))
    fill(mh.at[1], (ha == hb * R + R - 1, -QUARTER))
    down = sb - sa
    step_down = jnp.where((sa & (R - 1)) == R - 1, R + 1, 1)
    step_up = jnp.where((sa & (R - 1)) == 0, -(R + 1), -1)
    fill(mf, (down == step_down, -QUARTER), (down == step_up, -QUARTER))

    cond_copy.wait()
    for g in range(2):
        cnd = cond[0, pl.ds(pl.multiple_of(2 * R * h + g * R, R), R), :]
        for q in range(H):
            fac1[g, q, 0] = orders[q].astype(F32) * (1.0 / (2.0 * H)) * cnd
    for q in range(4):
        fac2[q] = (orders[4 * h + q].astype(F32) * (1.0 / (2.0 * H)) * cond[0]).reshape(2 * n, 1, R, 128)

    jcopy.wait()
    for a in range(3):
        for b in range(3):

            def fold(t, _, a=a, b=b):
                both = jac[a, b, t, 0].astype(F32) + jac[a, b, t + HALF, 0].astype(F32)
                both = both * (2.0 / NT)
                rows = pl.ds(pl.multiple_of(t * R, R), R)
                jeff[0, a, b, rows, :] = both[:R]
                jeff[1, a, b, rows, :] = both[R:]
                return 0

            lax.fori_loop(0, HALF, fold, 0, unroll=8)

    MB = 256

    def forward(src, g):
        cells = jnp.concatenate([src[g, i].reshape(K, 128) for i in range(3)], axis=1)

        def body(m, _):
            rows = pl.ds(pl.multiple_of(m * MB, MB), MB)
            smp = jnp.dot(tf[rows, :], cells, preferred_element_type=F32)
            for b in range(3):
                total = jeff[g, 0, b, rows, :] * smp[:, :128]
                total = total + jeff[g, 1, b, rows, :] * smp[:, 128:256]
                total = total + jeff[g, 2, b, rows, :] * smp[:, 256:]
                wgt[g, rows, 128 * b:128 * b + 128] = total.astype(BF16)
            return 0

        lax.fori_loop(0, K // MB, body, 0)

    def backward(g, dst, keep):
        def body(m, _):
            rows = pl.ds(pl.multiple_of(m * MB, MB), MB)
            pairs = pl.ds(m * (MB // R // 2), MB // R // 2)
            coef = jnp.dot(tb[rows, :], wgt[g], preferred_element_type=F32)
            for i in range(3):
                part = coef[:, 128 * i:128 * i + 128]
                if keep:
                    cf[i, rows, :] = part
                dst[g, i, pairs] = part.astype(BF16).reshape(MB // R // 2, 2 * R, 128)
            return 0

        lax.fori_loop(0, K // MB, body, 0)

    def xhalo(d, dst):
        return rdma(xs.at[d], xr.at[d], x_s.at[d], x_r.at[d], (p, dst))

    def zsend(g, i, d):
        if d == 0:
            return rdma(c1.at[g, i], zm.at[g, i], z_s.at[0, g, i], z_r.at[0, g, i], (mate, h))
        return rdma(c1.at[g, i], zo.at[g, i], z_s.at[1, g, i], z_r.at[1, g, i], (outer, h))

    def feed(kind, g, dx):
        dst = at(dx, hy) if kind < 2 else flip_dst(dx)
        src = (c1, zo, zo, c1)[kind]
        to = r1 if kind in (0, 2) else e1
        return rdma(
            src.at[g, :, pl.ds(4 * dst, 4)], to.at[2 * h + g], f_s.at[kind, g, dx], f_r.at[kind, g, dx],
            (p if kind < 2 else outer, dst),
        )

    def feed_end(g, dx):
        dst = flip_dst(dx)
        return rdma(
            c1.at[g, :, pl.ds(4 * dst, 4)], r1.at[2 * h + g], f_s.at[2, g, dx], f_r.at[2, g, dx], (p, dst)
        )

    for g in range(2):
        for dx in DIRECT:
            a2a(g, dx).wait_recv()
        for dx in FLIPS:
            a2a_flip(g, dx).wait_recv()
        forward(x1, g)
        backward(g, c1, True)

        @pl.when(has_outer)
        def _():
            for i in range(3):
                zsend(g, i, 1).start()

        for i in range(3):
            zsend(g, i, 0).start()

        for i in range(3):
            xs[g, i] = cf[i, pl.ds(0 if g == 0 else R - 1, C, stride=R), :].astype(BF16)

        if g == 0:

            @pl.when(h > 0)
            def _():
                xhalo(0, h - 1).start()

        else:

            @pl.when(h < n - 1)
            def _():
                xhalo(1, h + 1).start()

        @pl.when(has_outer)
        def _():
            for dx in range(4):
                feed(3, g, dx).start()

        @pl.when(jnp.logical_not(has_outer))
        def _():
            for dx in range(4):
                feed_end(g, dx).start()

        for dx in DIRECT:
            feed(0, g, dx).start()
        r1[2 * h + g] = c1[g, :, pl.ds(4 * h, 4)]

    def swapped(v, factor):
        return jnp.concatenate([factor * v[:, 1:], -(factor * v[:, :1])], axis=1)

    for g in range(2):
        has_x = h > 0 if g == 0 else h < n - 1

        @pl.when(has_x)
        def _():
            xhalo(1 - g, h).wait_recv()

        @pl.when(jnp.logical_not(has_x))
        def _():
            xr[1 - g] = jnp.zeros_like(xr[1 - g])

        for i in range(3):

            @pl.when(has_outer)
            def _():
                zsend(g, i, 1).wait_recv()

            @pl.when(jnp.logical_not(has_outer))
            def _():
                zo[g, i] = jnp.zeros_like(zo[g, i])

            zsend(g, i, 0).wait_recv()

            def first(b, _, g=g, i=i):
                pairs = pl.ds(16 * b, 16)
                mine = c1[g, i, pairs].reshape(256, 128)
                other = c1[1 - g, i, pairs].reshape(256, 128)
                halo = xr[1 - g, i, pl.ds(pl.multiple_of(32 * b, 32), 32), :]
                total = jnp.dot(mine, my[...], preferred_element_type=F32)
                total = total + jnp.dot(ms[...], mine, preferred_element_type=F32)
                total = total + jnp.dot(mc[g], other, preferred_element_type=F32)
                total = total + jnp.dot(mh[g], halo, preferred_element_type=F32)
                axial = zm[g, i, pairs].astype(F32) + zo[g, i, pairs].astype(F32)
                eddy = swapped(x1[g, i, pairs].astype(F32).reshape(16, 2, R, 128), fac1[g, pairs])
                total = total.reshape(16, 2 * R, 128) - QUARTER * axial + eddy.reshape(16, 2 * R, 128)
                x2[g, i, pairs] = total.astype(BF16)
                return 0

            lax.fori_loop(0, 2, first, 0)

        @pl.when(has_outer)
        def _():
            for dx in range(4):
                feed(2, g, dx).start()
            for dx in DIRECT:
                feed(1, g, dx).start()
            e1[2 * h + g] = zo[g, :, pl.ds(4 * h, 4)]

        @pl.when(jnp.logical_not(has_outer))
        def _():
            for k in range(n):
                e1[2 * k + g] = jnp.zeros_like(e1[2 * k + g])

        forward(x2, g)
        backward(g, c2, False)

    def own(i, dx):
        dst = at(dx, hy)
        return rdma(
            c2.at[:, i, pl.ds(4 * dst, 4)], r2.at[pl.ds(2 * h, 2), i], o_s.at[i, dx], o_r.at[i, dx], (p, dst)
        )

    def own_flip(i, dx):
        dst = flip_dst(dx)
        return rdma(
            c2.at[:, i, pl.ds(4 * dst, 4)], r2.at[pl.ds(2 * h, 2), i], fc_s.at[i, dx], fc_r.at[i, dx], (p, dst)
        )

    def edge(i, k):
        dst = peer(k)
        return rdma(
            c2.at[:, i, pl.ds(4 * dst, 4)], e2.at[pl.ds(2 * h, 2), i], e_s.at[i, k], e_r.at[i, k], (outer, dst)
        )

    def to_mate(i):
        return rdma(r2.at[:, i], m2.at[:, i], m_s.at[i], m_r.at[i], (mate, h))

    for i in range(3):
        for dx in FLIPS:
            own_flip(i, dx).start()
        for dx in DIRECT:
            own(i, dx).start()

        @pl.when(has_outer)
        def _():
            for k in (4, 5, 3, 1, 7, 2, 6, 0):
                edge(i, k).start()

    for g in range(2):
        r2[2 * h + g] = c2[g, :, pl.ds(4 * h, 4)]


    def finish(r, e, m, v, out, i):
        for q in range(4):
            mine = r[:, i, q].reshape(256, 128)
            total = jnp.dot(mine, my[...], preferred_element_type=F32)
            total = total + jnp.dot(mf[...], mine, preferred_element_type=F32)
            axial = e[:, i, q].astype(F32) + m[:, i, q].astype(F32)
            total = (total.reshape(2 * n, 2 * R, 128) - QUARTER * axial).reshape(2 * n, 2, R, 128)
            factor = fac2[q].reshape(2 * n * R, 128)
            out[2 * q, i, 0] = total[:, 0].reshape(2 * n * R, 128) + factor * v[2 * q + 1, i, 0]
            out[2 * q + 1, i, 0] = total[:, 1].reshape(2 * n * R, 128) - factor * v[2 * q, i, 0]

    def first_to_mate(i):
        return rdma(r1.at[:, i], m1.at[:, i], n_s.at[i], n_r.at[i], (mate, h))

    for g in range(2):
        for dx in DIRECT:
            feed(0, g, dx).wait_recv()
        for dx in range(4):
            feed_end(g, dx).wait_recv()
    for i in range(3):
        first_to_mate(i).start()

    @pl.when(has_outer)
    def _():
        for g in range(2):
            for dx in DIRECT:
                feed(1, g, dx).wait_recv()
            for dx in range(4):
                feed(3, g, dx).wait_recv()

    for i in range(3):
        first_to_mate(i).wait_recv()
        finish(r1, e1, m1, adj, out1, i)

    def finish_second(i):
        @pl.when(has_outer)
        def _():
            for k in range(n):
                edge(i, k).wait_recv()

        @pl.when(jnp.logical_not(has_outer))
        def _():
            e2[:, i] = jnp.zeros_like(e2[:, i])

        to_mate(i).wait_recv()
        finish(r2, e2, m2, out1, out2, i)

    for i in range(3):
        for dx in DIRECT:
            own(i, dx).wait_recv()
        for dx in FLIPS:
            own_flip(i, dx).wait_recv()
        to_mate(i).start()
        if i > 0:
            finish_second(i - 1)
    finish_second(2)

    for g in range(2):
        for dx in DIRECT:
            a2a(g, dx).wait_send()
            feed(0, g, dx).wait_send()
        for dx in FLIPS:
            a2a_flip(g, dx).wait_send()
        for dx in range(4):
            feed_end(g, dx).wait_send()

        @pl.when(has_outer)
        def _():
            for dx in DIRECT:
                feed(1, g, dx).wait_send()
            for dx in range(4):
                feed(3, g, dx).wait_send()

    @pl.when(h > 0)
    def _():
        xhalo(0, h - 1).wait_send()

    @pl.when(h < n - 1)
    def _():
        xhalo(1, h + 1).wait_send()

    for i in range(3):

        for g in range(2):
            zsend(g, i, 0).wait_send()

        @pl.when(has_outer)
        def _():
            for g in range(2):
                zsend(g, i, 1).wait_send()

        first_to_mate(i).wait_send()
        for dx in DIRECT:
            own(i, dx).wait_send()
        for dx in FLIPS:
            own_flip(i, dx).wait_send()

        @pl.when(has_outer)
        def _():
            for k in range(n):
                edge(i, k).wait_send()

        to_mate(i).wait_send()


def shards(adjoint, jacobian, conductivity, harm_order):
    n = lax.axis_size("harm")
    hbm = pl.BlockSpec(memory_space=pltpu.HBM)
    vmem = pl.BlockSpec(memory_space=pltpu.VMEM)
    pinned = [pltpu.with_memory_space_constraint(v, pltpu.HBM) for v in (adjoint, jacobian, conductivity, harm_order)]
    shape = jax.ShapeDtypeStruct(adjoint.shape, F32)
    by_rows = (2, 3, C // 2, 2 * R, 128)
    by_coeffs = (2 * n, 3, C // 2 // n, 2 * R, 128)
    dma = pltpu.SemaphoreType.DMA
    return pl.pallas_call(
        kernel,
        out_shape=(shape, shape),
        in_specs=[hbm, hbm, hbm, hbm],
        out_specs=(vmem, vmem),
        scratch_shapes=[
            pltpu.VMEM(adjoint.shape, F32),
            pltpu.VMEM(conductivity.shape, F32),
            pltpu.SMEM(harm_order.shape, jnp.int32),
            pltpu.VMEM((C, 128), jnp.int32),
            pltpu.VMEM(by_coeffs, BF16),
            pltpu.VMEM(by_rows, BF16),
            pltpu.VMEM(jacobian.shape, BF16),
            pltpu.VMEM((2, 3, 3, K, 128), F32),
            pltpu.VMEM((K, K), BF16),
            pltpu.VMEM((K, K), BF16),
            pltpu.VMEM((2, K, 3 * 128), BF16),
            pltpu.VMEM((3, K, 128), F32),
            pltpu.VMEM(by_rows, BF16),
            pltpu.VMEM(by_rows, BF16),
            pltpu.VMEM(by_rows, BF16),
            pltpu.VMEM((2, 3, C, 128), BF16),
            pltpu.VMEM((2, 3, C, 128), BF16),
            pltpu.VMEM(by_rows, BF16),
            pltpu.VMEM(by_coeffs, BF16),
            pltpu.VMEM(by_coeffs, BF16),
            pltpu.VMEM(by_coeffs, BF16),
            pltpu.VMEM(by_rows, BF16),
            pltpu.VMEM(by_coeffs, BF16),
            pltpu.VMEM(by_coeffs, BF16),
            pltpu.VMEM(by_coeffs, BF16),
            pltpu.VMEM((2, H, 1, R, 128), F32),
            pltpu.VMEM((4, 2 * n, 1, R, 128), F32),
            pltpu.VMEM((128, 128), BF16),
            pltpu.VMEM((256, 256), BF16),
            pltpu.VMEM((2, 256, 256), BF16),
            pltpu.VMEM((2, 256, 32), BF16),
            pltpu.VMEM((256, 256), BF16),
            dma, dma((4,)), dma, dma,
            dma((2, n)), dma((2, n)),
            dma((2, 2, 3)), dma((2, 2, 3)),
            dma((2,)), dma((2,)),
            dma((4, 2, 4)), dma((4, 2, 4)),
            dma((3, n)), dma((3, n)),
            dma((3, n)), dma((3, n)),
            dma((3,)), dma((3,)),
            dma((2, 4)), dma((2, 4)),
            dma((3, 4)), dma((3, 4)),
            dma((3,)), dma((3,)),
        ],
        compiler_params=pltpu.CompilerParams(
            collective_id=0, has_side_effects=True, vmem_limit_bytes=48 * 1024 * 1024
        ),
    )(*pinned)


def solution(mesh):
    return jax.shard_map(
        shards,
        mesh=mesh,
        in_specs=(
            P("harm", None, "slab", None, None),
            P(None, None, None, "slab", "harm", None),
            P("slab", None, None),
            P(),
        ),
        out_specs=(P("harm", None, "slab", None, None), P("harm", None, "slab", None, None)),
        check_vma=False,
    )
```

time: 147 us -> 74.3 us (0.51)
  Pallas kernels: 0 us -> 71.2 us
  waiting for transfers between devices: 47.1 us -> 0 us
  local copies, waits for them, and re-layouts: 29.8 us -> 2.29 us
  blocking collectives: 26.8 us -> 0 us
  starting transfers between devices: 25.5 us -> 0 us
  other arithmetic: 12.8 us -> 0 us
  matrix products: 3.64 us -> 0 us
    pallas_call x0 -> x1, Pallas kernels: none -> 71.2 us  [shards(): pl.pallas_call(kernel, out_shape=(shape, shape), in_specs=[hbm, hbm, hbm,...]
    ppermute x4 -> x0, waiting for transfers between devices: 34.7 us -> none  [the longest x2 34.7 us: padded_2(): lax.ppermute(head, axis, [((i + 1) % count, i) for i in range(ends)])]
    all_to_all x2 -> x0, blocking collectives: 26.8 us -> none  [the longest x1 14 us: transposed_apply(): lax.all_to_all(packed, 'harm', split_axis=3, concat_axis=0, tiled=True)]
    unnamed x24 -> x2, local copies, waits for them, and re-layouts: 20 us -> 2.29 us
    all_to_all x2 -> x0, starting transfers between devices: 13.4 us -> none  [the longest x1 6.77 us: transposed_apply(): lax.all_to_all(coeffs, 'harm', split_axis=0, concat_axis=3, tiled=True)]
    all_to_all x2 -> x0, waiting for transfers between devices: 12.4 us -> none  [the longest x1 12.4 us: transposed_apply(): lax.all_to_all(coeffs, 'harm', split_axis=0, concat_axis=3, tiled=True)]
    ppermute x4 -> x0, starting transfers between devices: 12.1 us -> none  [the longest x2 6.38 us: padded_2(): lax.ppermute(tail, axis, [(i, (i + 1) % count) for i in range(ends)])]
    another operation x8 -> x0, other arithmetic: 8.34 us -> none
  transfers between devices with their start and end apart: 6 -> 0, of which waited for: 3 -> 0; matrix products, arithmetic and copies ran while one was open for 14% -> 0% of each run, Pallas kernels for 0% -> 0%
where the time goes in v1:
time: 74.3 us; the launch traced here: 74.2 us
  Pallas kernels  71.2 us (96%)
  local copies, waits for them, and re-layouts  2.29 us (3%)
    pallas_call x1, Pallas kernels, shards(): pl.pallas_call(kernel, out_shape=(shape, shape), in_specs=[hbm, hbm, hbm,...  71.2 us
    unnamed x2, local copies, waits for them, and re-layouts  2.29 us

profile of v1, /device:TPU:225, one launch (start us, length us, event | category | flops | bytes accessed | tf_op | source)
XLA Modules:
  0.0 74.2 jit_solution(11573259142068411763)
XLA Ops:
  0.6 71.2 %shard_map.59 = (f32[8,3,1,128,128]{4,3,2,1,0:T(8,128)S(1)}, f32[8,3,1,128,128]{4,3,2,1,0:T(8,128)S(1)}) custom-call(f32[8,3,1,128,128]{4,3,2,1,0:T(8,128)} %adj_hbm.1, bf16[3,3,128,1,16,128]{5,4,3,2,1,0:T(8,128)(2,1)} %jac_hbm.1, f32[1,128,128]{2,1,0:T(8,128)} %cond_hbm.1, s32[32]{0:T(128)} %orders_hbm.1), custom_call_target="tpu_custom_call" | custom-call | tf_op jit(solution)/shard_map/pallas_call | solution.py:487
  71.9 1.1 %copy.8 = f32[8,3,1,128,128]{4,3,2,1,0:T(8,128)} copy(f32[8,3,1,128,128]{4,3,2,1,0:T(8,128)S(1)} %get-tuple-element.4) | data formatting | bytes 3145728
  73.0 1.1 %copy.9 = f32[8,3,1,128,128]{4,3,2,1,0:T(8,128)} copy(f32[8,3,1,128,128]{4,3,2,1,0:T(8,128)S(1)} %get-tuple-element.5) | data formatting | bytes 3145728

commit v2 on v1

--- a/solution.py
+++ b/solution.py
@@ -32,8 +32,8 @@
     n = lax.axis_size("harm")
     odd = lax.rem(p, 2)
     mate = p + 1 - 2 * odd
-    outer = p - 1 + 2 * odd
-    has_outer = jnp.logical_and(outer >= 0, outer < planes)
+    outer = lax.rem(p - 1 + 2 * odd + planes, planes)
+    inside = jnp.logical_and(p > 0, p < planes - 1).astype(F32)
 
     def peer(k):
         return lax.rem(h + k, n)
@@ -72,10 +72,8 @@
         pl.semaphore_signal(barrier, inc=1, device_id=(p, peer(k)), device_id_type=MESH)
     pl.semaphore_signal(barrier, inc=1, device_id=(mate, h), device_id_type=MESH)
 
-    @pl.when(has_outer)
-    def _():
-        for k in range(n):
-            pl.semaphore_signal(barrier, inc=1, device_id=(outer, peer(k)), device_id_type=MESH)
+    for k in range(n):
+        pl.semaphore_signal(barrier, inc=1, device_id=(outer, peer(k)), device_id_type=MESH)
 
     for q in range(4):
         adj_copy(q).wait()
@@ -89,7 +87,7 @@
 
         lax.fori_loop(0, 2 * n, pack, 0, unroll=4)
 
-    pl.semaphore_wait(barrier, n + n * has_outer.astype(jnp.int32))
+    pl.semaphore_wait(barrier, 2 * n)
 
     def a2a(g, dx):
         dst = at(dx, hy)
@@ -129,7 +127,6 @@
 
     spread((((1,), (1,)), ((), ())), tf)
     spread((((1,), (0,)), ((), ())), tb)
-
 
     QUARTER = 0.25
 
@@ -220,14 +217,8 @@
         src = (c1, zo, zo, c1)[kind]
         to = r1 if kind in (0, 2) else e1
         return rdma(
-            src.at[g, :, pl.ds(4 * dst, 4)], to.at[2 * h + g], f_s.at[kind, g, dx], f_r.at[kind, g, dx],
+            src.at[g, :, pl.ds(4 * dst, 4)], to.at[g, h], f_s.at[kind, g, dx], f_r.at[kind, g, dx],
             (p if kind < 2 else outer, dst),
-        )
-
-    def feed_end(g, dx):
-        dst = flip_dst(dx)
-        return rdma(
-            c1.at[g, :, pl.ds(4 * dst, 4)], r1.at[2 * h + g], f_s.at[2, g, dx], f_r.at[2, g, dx], (p, dst)
         )
 
     for g in range(2):
@@ -238,10 +229,8 @@
         forward(x1, g)
         backward(g, c1, True)
 
-        @pl.when(has_outer)
-        def _():
-            for i in range(3):
-                zsend(g, i, 1).start()
+        for i in range(3):
+            zsend(g, i, 1).start()
 
         for i in range(3):
             zsend(g, i, 0).start()
@@ -261,19 +250,37 @@
             def _():
                 xhalo(1, h + 1).start()
 
-        @pl.when(has_outer)
-        def _():
-            for dx in range(4):
-                feed(3, g, dx).start()
-
-        @pl.when(jnp.logical_not(has_outer))
-        def _():
-            for dx in range(4):
-                feed_end(g, dx).start()
+        for dx in range(4):
+            feed(3, g, dx).start()
 
         for dx in DIRECT:
             feed(0, g, dx).start()
-        r1[2 * h + g] = c1[g, :, pl.ds(4 * h, 4)]
+        r1[g, h] = c1[g, :, pl.ds(4 * h, 4)]
+
+    def own(g, dx):
+        dst = at(dx, hy)
+        return rdma(c2.at[g, :, pl.ds(4 * dst, 4)], r2.at[g, h], o_s.at[g, dx], o_r.at[g, dx], (p, dst))
+
+    def own_flip(g, dx):
+        dst = flip_dst(dx)
+        return rdma(c2.at[g, :, pl.ds(4 * dst, 4)], r2.at[g, h], fc_s.at[g, dx], fc_r.at[g, dx], (p, dst))
+
+    def edge(g, k):
+        dst = peer(k)
+        return rdma(c2.at[g, :, pl.ds(4 * dst, 4)], e2.at[g, h], e_s.at[g, k], e_r.at[g, k], (outer, dst))
+
+    def to_mate(g, i):
+        return rdma(r2.at[g, :, i], m2.at[g, :, i], m_s.at[g, i], m_r.at[g, i], (mate, h))
+
+    def exchange(g):
+        for dx in FLIPS:
+            own_flip(g, dx).start()
+
+        for k in (4, 5, 3, 1, 7, 2, 6, 0):
+            edge(g, k).start()
+
+        for dx in DIRECT:
+            own(g, dx).start()
 
     def swapped(v, factor):
         return jnp.concatenate([factor * v[:, 1:], -(factor * v[:, :1])], axis=1)
@@ -291,15 +298,12 @@
 
         for i in range(3):
 
-            @pl.when(has_outer)
-            def _():
-                zsend(g, i, 1).wait_recv()
-
-            @pl.when(jnp.logical_not(has_outer))
-            def _():
-                zo[g, i] = jnp.zeros_like(zo[g, i])
+            zsend(g, i, 1).wait_recv()
 
             zsend(g, i, 0).wait_recv()
+
+            if g == 1 and i == 2:
+                exchange(0)
 
             def first(b, _, g=g, i=i):
                 pairs = pl.ds(16 * b, 16)
@@ -310,7 +314,7 @@
                 total = total + jnp.dot(ms[...], mine, preferred_element_type=F32)
                 total = total + jnp.dot(mc[g], other, preferred_element_type=F32)
                 total = total + jnp.dot(mh[g], halo, preferred_element_type=F32)
-                axial = zm[g, i, pairs].astype(F32) + zo[g, i, pairs].astype(F32)
+                axial = zm[g, i, pairs].astype(F32) + inside * zo[g, i, pairs].astype(F32)
                 eddy = swapped(x1[g, i, pairs].astype(F32).reshape(16, 2, R, 128), fac1[g, pairs])
                 total = total.reshape(16, 2 * R, 128) - QUARTER * axial + eddy.reshape(16, 2 * R, 128)
                 x2[g, i, pairs] = total.astype(BF16)
@@ -318,114 +322,81 @@
 
             lax.fori_loop(0, 2, first, 0)
 
-        @pl.when(has_outer)
-        def _():
-            for dx in range(4):
-                feed(2, g, dx).start()
-            for dx in DIRECT:
-                feed(1, g, dx).start()
-            e1[2 * h + g] = zo[g, :, pl.ds(4 * h, 4)]
-
-        @pl.when(jnp.logical_not(has_outer))
-        def _():
-            for k in range(n):
-                e1[2 * k + g] = jnp.zeros_like(e1[2 * k + g])
+        for dx in range(4):
+            feed(2, g, dx).start()
+        for dx in DIRECT:
+            feed(1, g, dx).start()
+        e1[g, h] = zo[g, :, pl.ds(4 * h, 4)]
 
         forward(x2, g)
         backward(g, c2, False)
 
-    def own(i, dx):
-        dst = at(dx, hy)
-        return rdma(
-            c2.at[:, i, pl.ds(4 * dst, 4)], r2.at[pl.ds(2 * h, 2), i], o_s.at[i, dx], o_r.at[i, dx], (p, dst)
-        )
-
-    def own_flip(i, dx):
-        dst = flip_dst(dx)
-        return rdma(
-            c2.at[:, i, pl.ds(4 * dst, 4)], r2.at[pl.ds(2 * h, 2), i], fc_s.at[i, dx], fc_r.at[i, dx], (p, dst)
-        )
-
-    def edge(i, k):
-        dst = peer(k)
-        return rdma(
-            c2.at[:, i, pl.ds(4 * dst, 4)], e2.at[pl.ds(2 * h, 2), i], e_s.at[i, k], e_r.at[i, k], (outer, dst)
-        )
-
-    def to_mate(i):
-        return rdma(r2.at[:, i], m2.at[:, i], m_s.at[i], m_r.at[i], (mate, h))
-
-    for i in range(3):
-        for dx in FLIPS:
-            own_flip(i, dx).start()
-        for dx in DIRECT:
-            own(i, dx).start()
-
-        @pl.when(has_outer)
-        def _():
-            for k in (4, 5, 3, 1, 7, 2, 6, 0):
-                edge(i, k).start()
-
-    for g in range(2):
-        r2[2 * h + g] = c2[g, :, pl.ds(4 * h, 4)]
-
-
-    def finish(r, e, m, v, out, i):
+    exchange(1)
+    for g in range(2):
+        r2[g, h] = c2[g, :, pl.ds(4 * h, 4)]
+
+    def rows(ref, i, q):
+        return jnp.stack([ref[0, :, i, q], ref[1, :, i, q]], axis=1).reshape(2 * n, 2 * R, 128)
+
+    def inplane(r, v, out, i):
         for q in range(4):
-            mine = r[:, i, q].reshape(256, 128)
+            mine = rows(r, i, q).reshape(256, 128)
             total = jnp.dot(mine, my[...], preferred_element_type=F32)
             total = total + jnp.dot(mf[...], mine, preferred_element_type=F32)
-            axial = e[:, i, q].astype(F32) + m[:, i, q].astype(F32)
-            total = (total.reshape(2 * n, 2 * R, 128) - QUARTER * axial).reshape(2 * n, 2, R, 128)
+            total = total.reshape(2 * n, 2, R, 128)
             factor = fac2[q].reshape(2 * n * R, 128)
             out[2 * q, i, 0] = total[:, 0].reshape(2 * n * R, 128) + factor * v[2 * q + 1, i, 0]
             out[2 * q + 1, i, 0] = total[:, 1].reshape(2 * n * R, 128) - factor * v[2 * q, i, 0]
 
-    def first_to_mate(i):
-        return rdma(r1.at[:, i], m1.at[:, i], n_s.at[i], n_r.at[i], (mate, h))
+    def axial(e, m, out, i):
+        for q in range(4):
+            both = QUARTER * (inside * rows(e, i, q).astype(F32) + rows(m, i, q).astype(F32))
+            both = both.reshape(2 * n, 2, R, 128)
+            out[2 * q, i, 0] = out[2 * q, i, 0] - both[:, 0].reshape(2 * n * R, 128)
+            out[2 * q + 1, i, 0] = out[2 * q + 1, i, 0] - both[:, 1].reshape(2 * n * R, 128)
+
+    def first_to_mate(g):
+        return rdma(r1.at[g], m1.at[g], n_s.at[g], n_r.at[g], (mate, h))
 
     for g in range(2):
         for dx in DIRECT:
             feed(0, g, dx).wait_recv()
         for dx in range(4):
-            feed_end(g, dx).wait_recv()
+            feed(2, g, dx).wait_recv()
+        first_to_mate(g).start()
+
     for i in range(3):
-        first_to_mate(i).start()
-
-    @pl.when(has_outer)
-    def _():
+        inplane(r1, adj, out1, i)
+
+    for g in range(2):
+        for dx in DIRECT:
+            feed(1, g, dx).wait_recv()
+        for dx in range(4):
+            feed(3, g, dx).wait_recv()
+
+    for g in range(2):
+        first_to_mate(g).wait_recv()
+    for i in range(3):
+        axial(e1, m1, out1, i)
+
+    for g in range(2):
+        for dx in DIRECT:
+            own(g, dx).wait_recv()
+        for dx in FLIPS:
+            own_flip(g, dx).wait_recv()
+        for i in range(3):
+            to_mate(g, i).start()
+    for i in range(3):
+        inplane(r2, out1, out2, i)
+
+    for g in range(2):
+        for k in range(n):
+            edge(g, k).wait_recv()
+
+    for i in range(3):
         for g in range(2):
-            for dx in DIRECT:
-                feed(1, g, dx).wait_recv()
-            for dx in range(4):
-                feed(3, g, dx).wait_recv()
-
-    for i in range(3):
-        first_to_mate(i).wait_recv()
-        finish(r1, e1, m1, adj, out1, i)
-
-    def finish_second(i):
-        @pl.when(has_outer)
-        def _():
-            for k in range(n):
-                edge(i, k).wait_recv()
-
-        @pl.when(jnp.logical_not(has_outer))
-        def _():
-            e2[:, i] = jnp.zeros_like(e2[:, i])
-
-        to_mate(i).wait_recv()
-        finish(r2, e2, m2, out1, out2, i)
-
-    for i in range(3):
-        for dx in DIRECT:
-            own(i, dx).wait_recv()
-        for dx in FLIPS:
-            own_flip(i, dx).wait_recv()
-        to_mate(i).start()
-        if i > 0:
-            finish_second(i - 1)
-    finish_second(2)
+            to_mate(g, i).wait_recv()
+        axial(e2, m2, out2, i)
 
     for g in range(2):
         for dx in DIRECT:
@@ -434,14 +405,12 @@
         for dx in FLIPS:
             a2a_flip(g, dx).wait_send()
         for dx in range(4):
-            feed_end(g, dx).wait_send()
-
-        @pl.when(has_outer)
-        def _():
-            for dx in DIRECT:
-                feed(1, g, dx).wait_send()
-            for dx in range(4):
-                feed(3, g, dx).wait_send()
+            feed(2, g, dx).wait_send()
+
+        for dx in DIRECT:
+            feed(1, g, dx).wait_send()
+        for dx in range(4):
+            feed(3, g, dx).wait_send()
 
     @pl.when(h > 0)
     def _():
@@ -456,23 +425,23 @@
         for g in range(2):
             zsend(g, i, 0).wait_send()
 
-        @pl.when(has_outer)
-        def _():
-            for g in range(2):
-                zsend(g, i, 1).wait_send()
-
-        first_to_mate(i).wait_send()
-        for dx in DIRECT:
-            own(i, dx).wait_send()
+        for g in range(2):
+            zsend(g, i, 1).wait_send()
+
+    for g in range(2):
+        first_to_mate(g).wait_send()
+
+    for g in range(2):
+        for dx in DIRECT:
+            own(g, dx).wait_send()
         for dx in FLIPS:
-            own_flip(i, dx).wait_send()
-
-        @pl.when(has_outer)
-        def _():
-            for k in range(n):
-                edge(i, k).wait_send()
-
-        to_mate(i).wait_send()
+            own_flip(g, dx).wait_send()
+
+        for k in range(n):
+            edge(g, k).wait_send()
+
+        for i in range(3):
+            to_mate(g, i).wait_send()
 
 
 def shards(adjoint, jacobian, conductivity, harm_order):
@@ -482,7 +451,8 @@
     pinned = [pltpu.with_memory_space_constraint(v, pltpu.HBM) for v in (adjoint, jacobian, conductivity, harm_order)]
     shape = jax.ShapeDtypeStruct(adjoint.shape, F32)
     by_rows = (2, 3, C // 2, 2 * R, 128)
-    by_coeffs = (2 * n, 3, C // 2 // n, 2 * R, 128)
+    tile = (3, C // 2 // n, 2 * R, 128)
+    by_coeffs = (2, n) + tile
     dma = pltpu.SemaphoreType.DMA
     return pl.pallas_call(
         kernel,
@@ -494,7 +464,7 @@
             pltpu.VMEM(conductivity.shape, F32),
             pltpu.SMEM(harm_order.shape, jnp.int32),
             pltpu.VMEM((C, 128), jnp.int32),
-            pltpu.VMEM(by_coeffs, BF16),
+            pltpu.VMEM((2 * n,) + tile, BF16),
             pltpu.VMEM(by_rows, BF16),
             pltpu.VMEM(jacobian.shape, BF16),
             pltpu.VMEM((2, 3, 3, K, 128), F32),
@@ -527,12 +497,12 @@
             dma((2, 2, 3)), dma((2, 2, 3)),
             dma((2,)), dma((2,)),
             dma((4, 2, 4)), dma((4, 2, 4)),
-            dma((3, n)), dma((3, n)),
-            dma((3, n)), dma((3, n)),
-            dma((3,)), dma((3,)),
             dma((2, 4)), dma((2, 4)),
-            dma((3, 4)), dma((3, 4)),
-            dma((3,)), dma((3,)),
+            dma((2, n)), dma((2, n)),
+            dma((2, 3)), dma((2, 3)),
+            dma((2, 4)), dma((2, 4)),
+            dma((2, 4)), dma((2, 4)),
+            dma((2,)), dma((2,)),
         ],
         compiler_params=pltpu.CompilerParams(
             collective_id=0, has_side_effects=True, vmem_limit_bytes=48 * 1024 * 1024

time: 74.3 us -> 74.4 us (level)
  the two profiles are of different devices: /device:TPU:225 before, /device:TPU:25 now
where the time goes in v2:
time: 74.4 us
  Pallas kernels  71.4 us (96%)
  local copies, waits for them, and re-layouts  2.29 us (3%)
    pallas_call x1, Pallas kernels, shards(): pl.pallas_call(kernel, out_shape=(shape, shape), in_specs=[hbm, hbm, hbm,...  71.4 us
    unnamed x2, local copies, waits for them, and re-layouts  2.29 us

profile of v2, /device:TPU:25, one launch (start us, length us, event | category | flops | bytes accessed | tf_op | source)
XLA Modules:
  0.0 74.4 jit_solution(17936024725085513275)
XLA Ops:
  0.6 71.4 %shard_map.59 = (f32[8,3,1,128,128]{4,3,2,1,0:T(8,128)S(1)}, f32[8,3,1,128,128]{4,3,2,1,0:T(8,128)S(1)}) custom-call(f32[8,3,1,128,128]{4,3,2,1,0:T(8,128)} %adj_hbm.1, bf16[3,3,128,1,16,128]{5,4,3,2,1,0:T(8,128)(2,1)} %jac_hbm.1, f32[1,128,128]{2,1,0:T(8,128)} %cond_hbm.1, s32[32]{0:T(128)} %orders_hbm.1), custom_call_target="tpu_custom_call" | custom-call | tf_op jit(solution)/shard_map/pallas_call | solution.py:457
  72.1 1.1 %copy.8 = f32[8,3,1,128,128]{4,3,2,1,0:T(8,128)} copy(f32[8,3,1,128,128]{4,3,2,1,0:T(8,128)S(1)} %get-tuple-element.4) | data formatting | bytes 3145728
  73.2 1.1 %copy.9 = f32[8,3,1,128,128]{4,3,2,1,0:T(8,128)} copy(f32[8,3,1,128,128]{4,3,2,1,0:T(8,128)S(1)} %get-tuple-element.5) | data formatting | bytes 3145728

commit v3 on v2

--- a/solution.py
+++ b/solution.py
@@ -59,7 +59,7 @@
     hx, hy = h // 2, lax.rem(h, 2)
 
     def at(dx, y):
-        return 2 * lax.rem(hx + dx + 4, 4) + y
+        return 2 * lax.rem(hx + dx * (1 - 2 * lax.rem(hx, 2)) + 4, 4) + y
 
     def flip_dst(dx):
         return at(dx, 1 - hy)

time: 74.4 us -> 75.4 us (1.013)
  the two profiles are of different devices: /device:TPU:25 before, /device:TPU:27 now
where the time goes in v3:
time: 75.4 us; the launch traced here: 75.3 us
  Pallas kernels  72.4 us (96%)
  local copies, waits for them, and re-layouts  2.29 us (3%)
    pallas_call x1, Pallas kernels, shards(): pl.pallas_call(kernel, out_shape=(shape, shape), in_specs=[hbm, hbm, hbm,...  72.4 us
    unnamed x2, local copies, waits for them, and re-layouts  2.29 us

profile of v3, /device:TPU:27, one launch (start us, length us, event | category | flops | bytes accessed | tf_op | source)
XLA Modules:
  0.0 75.3 jit_solution(13127630374169460170)
XLA Ops:
  0.6 72.4 %shard_map.59 = (f32[8,3,1,128,128]{4,3,2,1,0:T(8,128)S(1)}, f32[8,3,1,128,128]{4,3,2,1,0:T(8,128)S(1)}) custom-call(f32[8,3,1,128,128]{4,3,2,1,0:T(8,128)} %adj_hbm.1, bf16[3,3,128,1,16,128]{5,4,3,2,1,0:T(8,128)(2,1)} %jac_hbm.1, f32[1,128,128]{2,1,0:T(8,128)} %cond_hbm.1, s32[32]{0:T(128)} %orders_hbm.1), custom_call_target="tpu_custom_call" | custom-call | tf_op jit(solution)/shard_map/pallas_call | solution.py:457
  73.0 1.1 %copy.8 = f32[8,3,1,128,128]{4,3,2,1,0:T(8,128)} copy(f32[8,3,1,128,128]{4,3,2,1,0:T(8,128)S(1)} %get-tuple-element.4) | data formatting | bytes 3145728
  74.2 1.1 %copy.9 = f32[8,3,1,128,128]{4,3,2,1,0:T(8,128)} copy(f32[8,3,1,128,128]{4,3,2,1,0:T(8,128)S(1)} %get-tuple-element.5) | data formatting | bytes 3145728
